TPU v7x, 32 devices: a whole 2x2x4 slice. The times are simulated.
32 devices in a mesh: grp: 2 (over y), seq: 4 (over z), head: 2 (over x), hold: 2 (over core).
Axes of the slice: x: 2, y: 2, z: 4, core: 2. Of those that a mesh axis runs over, the one named last changes fastest.
Arguments:
- meet_span: int32 [2], P('grp'), parts along dimension 0, may hold values from 2 to 6
- span_map: int32 [16], P('grp'), parts along dimension 0, may hold values from 0 to 7, each once
- hidden: bfloat16 [4096, 8192], P(('grp', 'seq')), parts along dimension 0, may hold values from -6 to 6
- w_query: bfloat16 [8192, 8, 512], P('seq', ('head', 'hold')), may hold values from -0.0625 to 0.0625
- w_keyval: bfloat16 [8192, 8, 256], P('seq', ('head', 'hold')), may hold values from -0.0625 to 0.0625
- stored_kv: bfloat16 [4096, 8, 256], P(('grp', 'seq'), ('head', 'hold')), parts along dimension 0, may hold values from -650 to 650, as said below
Outputs:
- attended: bfloat16 [4096, 8, 512], P(('grp', 'seq'), ('head', 'hold')), parts along dimension 0
- kv_cache: bfloat16 [4096, 8, 256], P(('grp', 'seq'), ('head', 'hold')), parts along dimension 0
There are 2 independent parts, one for each index of `grp`. A program takes and returns all parts, laid end to end along the dimension named above; an argument that names none is the same for every part. Nothing has to cross between parts.
Inputs may be any that keep to these rules, and one draw needn't show every extreme that they name: `stored_kv`: keys may be large on some rows.
All inputs are finite; a program needn't handle non-finite values.
Results may differ from a plain program's by a relative error of at most 0.012.
Values may be sent and summed in bfloat16 or wider, within the bound.
A program may use at most 128 MiB of HBM per device.

v0:
```python
import jax
import jax.numpy as jnp
from jax import lax
from jax.sharding import PartitionSpec as P

CH = 256


theta_base = 500000.0
lowest = -1e30


def rotate(values, positions):
    half_width = values.shape[-1] // 2
    frequency = theta_base ** (
        -(jnp.arange(half_width, dtype=jnp.float32) * 2.0) / values.shape[-1]
    )
    angles = positions.astype(jnp.float32)[:, None] * frequency[None, :]
    bcast_shape = (positions.shape[0],) + (1,) * (values.ndim - 2) + (half_width,)
    cosine = jnp.cos(angles).reshape(bcast_shape)
    sine_part = jnp.sin(angles).reshape(bcast_shape)
    lower_half = values[..., :half_width]
    upper_half = values[..., half_width:]
    return jnp.concatenate(
        [
            lower_half * cosine - upper_half * sine_part,
            upper_half * cosine + lower_half * sine_part,
        ],
        -1,
    )


def attend_block(
    carried, key_part, value_part, key_pos, own_queries, query_pos, is_live, score_scale
):

    def run_block(current):
        run_max, run_sum, run_acc = current
        scores = (
            jnp.einsum("ckgd,nkd->kgcn", own_queries, key_part, preferred_element_type=jnp.float32)
            * score_scale
        )
        allowed = key_pos[None, None, None, :] <= query_pos[None, None, :, None]
        scores = jnp.where(allowed, scores, lowest)
        new_max = jnp.maximum(run_max, scores.max(-1))
        weights = jnp.where(allowed, jnp.exp(scores - new_max[..., None]), 0.0)
        rescale = jnp.exp(run_max - new_max)
        run_acc = run_acc * rescale[..., None] + jnp.einsum(
            "kgcn,nkd->kgcd",
            weights.astype(jnp.bfloat16),
            value_part,
            preferred_element_type=jnp.float32,
        )
        run_sum = run_sum * rescale + weights.sum(-1)
        return (new_max, run_sum, run_acc)

    needed = is_live & (jnp.min(key_pos) <= jnp.max(query_pos))
    return lax.cond(needed, run_block, lambda current: current, carried)


def local(meet_span, span_map, hidden, w_query, w_keyval, stored_kv):
    row_count, features = hidden.shape
    span_count = span_map.shape[0]
    local_heads = w_query.shape[1]
    head_width = stored_kv.shape[2] // 2
    group_size = w_query.shape[2] // head_width
    span_len = CH
    slots_dev = row_count // span_len
    score_scale = head_width ** (-0.5)
    seq_index = lax.axis_index("seq")
    my_spans = lax.dynamic_slice_in_dim(span_map, seq_index * slots_dev, slots_dev, 0)
    offsets = jnp.arange(span_len, dtype=jnp.int32)
    positions = (my_spans[:, None] * span_len + offsets[None, :]).reshape(-1)
    computed_slot = (my_spans < meet_span[0]) | (my_spans == span_count - 1)
    whole_query, whole_keyval = (
        lax.all_gather(w_query, "seq", axis=0, tiled=True),
        lax.all_gather(w_keyval, "seq", axis=0, tiled=True),
    )
    query_raw = jnp.dot(
        hidden, whole_query.reshape(features, -1), preferred_element_type=jnp.float32
    )
    keyval_raw = jnp.dot(
        hidden, whole_keyval.reshape(features, -1), preferred_element_type=jnp.float32
    )
    queries = rotate(
        query_raw.reshape(row_count, local_heads, group_size, head_width), positions
    ).astype(jnp.bfloat16)
    keyval_raw = keyval_raw.reshape(row_count, local_heads, 2 * head_width)
    rotated = rotate(keyval_raw[..., :head_width], positions)
    recomputed = jnp.concatenate([rotated, keyval_raw[..., head_width:]], -1).astype(jnp.bfloat16)
    computed_rows = jnp.repeat(computed_slot, span_len)
    kv_cache = jnp.where(computed_rows[:, None, None], recomputed, stored_kv)
    slot_queries = queries.reshape(slots_dev, span_len, local_heads, group_size, head_width)
    slot_pos = positions.reshape(slots_dev, span_len)
    span_ids = jnp.arange(span_count, dtype=jnp.int32)

    def update_slots(carried, key_part, value_part, key_pos):
        return tuple(
            (
                attend_block(
                    carried[slot],
                    key_part,
                    value_part,
                    key_pos,
                    slot_queries[slot],
                    slot_pos[slot],
                    computed_slot[slot],
                    score_scale,
                )
                for slot in range(slots_dev)
            )
        )

    start_state = tuple(
        (
            (
                jnp.full((local_heads, group_size, span_len), lowest, jnp.float32),
                jnp.zeros((local_heads, group_size, span_len), jnp.float32),
                jnp.zeros((local_heads, group_size, span_len, head_width), jnp.float32),
            )
            for slot in range(slots_dev)
        )
    )
    portion = lax.all_gather(kv_cache, "seq", axis=0, tiled=True)
    piece_rows = portion.shape[0]
    key_ids = jnp.arange(piece_rows, dtype=jnp.int32)
    match = (key_ids // span_len)[:, None] == span_ids[None, :]
    key_span = jnp.sum(jnp.where(match, span_map[None, :], 0), 1)
    key_pos = key_span * span_len + key_ids % span_len
    key_block = min(piece_rows, 1024)
    block_count = piece_rows // key_block
    blocked = portion.reshape(block_count, key_block, local_heads, 2 * head_width)
    blocked_pos = key_pos.reshape(block_count, key_block)

    def scan_step(current, inputs):
        return (
            update_slots(
                current, inputs[0][..., :head_width], inputs[0][..., head_width:], inputs[1]
            ),
            None,
        )

    fold_result, _ = lax.scan(scan_step, start_state, (blocked, blocked_pos))
    outputs = []
    for slot in range(slots_dev):
        run_max, run_sum, run_acc = fold_result[slot]
        result = run_acc / jnp.where(run_sum > 0, run_sum, 1.0)[..., None]
        result = jnp.where(computed_slot[slot], result, 0.0)
        outputs.append(
            jnp.transpose(result, (2, 0, 1, 3)).reshape(
                span_len, local_heads, group_size * head_width
            )
        )
    attended = jnp.concatenate(outputs, 0).astype(jnp.bfloat16)
    return (attended, kv_cache)


def solution(mesh):
    return jax.shard_map(
        local,
        mesh=mesh,
        in_specs=(
            P("grp"),
            P("grp"),
            P(("grp", "seq"), None),
            P("seq", ("head", "hold"), None),
            P("seq", ("head", "hold"), None),
            P(("grp", "seq"), ("head", "hold"), None),
        ),
        out_specs=(
            P(("grp", "seq"), ("head", "hold"), None),
            P(("grp", "seq"), ("head", "hold"), None),
        ),
        check_vma=False,
    )
```

profile of v0, /device:TPU:0, one launch (start us, length us, event | category | flops | bytes accessed | tf_op | source)
XLA Modules:
  0.0 618.4 jit_solution(7581499056524458622)
XLA Ops:
  7.2 0.0 all-gather.4.cloned.1.call-start
  7.2 0.7 all-gather.4.cloned.1.call-update
  7.9 0.0 all-gather.6.cloned.1.call-start
  8.6 0.7 compare_or_fusion
  9.3 0.1 broadcast_in_dim.84
  9.4 0.7 broadcast_multiply_fusion.1
  10.2 0.1 convert_bitcast_fusion
  10.2 1.3 copy.33
  11.6 0.5 multiply_cosine_fusion
  12.1 149.8 %all-gather.4.cloned.1.call-done = bf16[8192,2,256]{2,1,0:T(2,128)(2,1)} async-done(((bf16[2048,2,256]{2,1,0:T(2,128)(2,1)}), bf16[8192,2,256]{2,1,0:T(2,128)(2,1)}) %all-gather.4.cloned.1.call-update) | async-done | bytes 8388624 | tf_op jit(solution)/shard_map/all_gather | solution.py:77
  161.9 21.2 %copy.48 = bf16[8192,2,256]{0,2,1:T(8,128)(2,1)} copy(bf16[8192,2,256]{2,1,0:T(2,128)(2,1)} %all-gather.4.cloned.1.call-done) | data formatting | bytes 16777216 | tf_op jit(solution)/shard_map/reshape | solution.py:83
  183.1 0.0 copy-start.2
  183.1 9.4 %fusion.38 = f32[512,2,256]{0,2,1:T(8,128)S(1)} fusion(bf16[8192,2,256]{0,2,1:T(8,128)(2,1)} %copy.48, bf16[512,8192]{1,0:T(8,128)(2,1)} %param.14), kind=kOutput, calls=%fused_computation.44 | convolution fusion | flops 4294967296 | bytes 17825792 | tf_op jit(solution)/shard_map/dot_general | solution.py:82
  192.6 0.1 subtract_convert_fusion.1
  192.7 0.9 maximum_select_fusion
  193.6 0.0 all-gather.6.cloned.1.call-update
  193.7 0.0 all-gather.8.cloned.1.call-start
  193.7 0.7 all-gather.8.cloned.1.call-update
  194.4 0.0 copy-done.2
  194.4 0.1 select_reduce_fusion
  194.5 0.7 slice_reduce_fusion
  195.2 0.6 fusion.51
  195.9 2.0 copy.40
  197.9 40.1 %all-gather.6.cloned.1.call-done = bf16[2048,2,256]{0,2,1:T(8,128)(2,1)} async-done(((bf16[512,2,256]{0,2,1:T(8,128)(2,1)}), bf16[2048,2,256]{0,2,1:T(8,128)(2,1)}) %all-gather.6.cloned.1.call-update) | async-done | bytes 2097168 | tf_op jit(solution)/shard_map/all_gather | solution.py:124
  238.0 3.3 reshape.247
  241.3 4.1 copy.37
  245.4 279.7 %all-gather.8.cloned.1.call-done = bf16[8192,2,512]{2,1,0:T(2,128)(2,1)} async-done(((bf16[2048,2,512]{2,1,0:T(2,128)(2,1)}), bf16[8192,2,512]{2,1,0:T(2,128)(2,1)}) %all-gather.8.cloned.1.call-update) | async-done | bytes 16777232 | tf_op jit(solution)/shard_map/all_gather | solution.py:76
  525.1 41.0 %copy.49 = bf16[8192,2,512]{0,2,1:T(8,128)(2,1)} copy(bf16[8192,2,512]{2,1,0:T(2,128)(2,1)} %all-gather.8.cloned.1.call-done) | data formatting | bytes 33554432 | tf_op jit(solution)/shard_map/reshape | solution.py:80
  566.1 14.2 %fusion.36 = f32[512,2,4,128]{0,3,2,1:T(8,128)S(1)} fusion(bf16[2,4,128,8192]{3,2,1,0:T(8,128)(2,1)} %bitcast.129, bf16[512,8192]{1,0:T(8,128)(2,1)} %param.14), kind=kOutput, calls=%fused_computation.42 | convolution fusion | flops 8589934592 | bytes 27262976 | tf_op jit(solution)/shard_map/dot_general | solution.py:79
  580.3 0.4 subtract_convert_fusion
  580.7 0.1 concatenate.18
  580.8 0.7 copy.35
  581.5 0.1 concatenate.19
  581.6 0.7 copy.36
  582.3 0.6 pad_maximum_fusion
  582.9 0.1 broadcast.211.clone
  583.0 1.1 broadcast.211
  584.1 21.2 %while.22 = (s32[]{:T(128)}, f32[2,4,256]{2,1,0:T(4,128)S(1)}, f32[2,4,256]{2,1,0:T(4,128)S(1)}, f32[2,4,256,128]{3,2,1,0:T(8,128)}, f32[2,4,256]{2,1,0:T(4,128)...) while((s32[]{:T(128)}, f32[2,4,256]{2,1,0:T(4,128)S(1)}, ...), condition=%wide.region_13.14_spmd.clone, body=%wide.region_3.13_spmd.clone.sunk | while | flops 2203592192 | bytes 72638960 | solution.py:143
  584.1 0.6 fusion.56
  584.7 0.1 iota_add_fusion.3
  584.7 0.7 fusion.57
  589.3 1.3 dynamic-slice_bitcast_fusion.2
  590.6 0.2 fusion.58
  590.8 7.7 %conditional.6 = ((f32[2,4,256]{2,1,0:T(4,128)S(1)}, f32[2,4,256]{2,1,0:T(4,128)S(1)}, f32[2,4,256,128]{3,2,1,0:T(8,128)})) conditional(s32[]{:T(128)} %convert_element_type.44, (f32[2,4,256]{2,1,0:T(4,128)S(1)}, f32[2,4,256]{2,1,0:T(4,128)S(1)}, f32[2,4,256,128]{3,2,1,0:T(8,128)}) %tuple.79, (s32[1024]{0:T(1024)S(1)}, s32[2,256]{1,0:T(2,128)S(1)}, ...), branch_computations={%region_5.5_spmd, %region_6.8_spmd} | conditional | flops 1101795328 | bytes 38411352 | solution.py:58
  590.8 0.2 broadcast_compare_fusion
  591.0 0.0 copy-start
  591.0 1.4 fusion.2
  592.4 2.0 fusion.4
  594.5 0.0 copy-done
  594.5 3.0 fusion.8
  597.5 0.0 copy-start.1
  597.5 1.0 copy-done.1
  598.5 0.6 fusion.56
  599.1 0.1 iota_add_fusion.3
  599.2 0.7 fusion.57
  603.7 1.3 dynamic-slice_bitcast_fusion.2
  605.0 0.2 fusion.58
  605.3 3.0 fusion.41
  608.3 0.4 copy.38
  608.7 0.2 reshape.249
  608.9 0.4 copy.39
  609.3 0.2 reshape.250
  609.5 2.3 pad_maximum_fusion.1
  (21 shorter events, 0.2 us)
Async XLA Ops:
  7.2 154.8 %all-gather.4.cloned.1.call-start = ((), (), s32[]{:S(2)}) async-start(), calls=%async_computation | async-start | bytes 10485760 | tf_op jit(solution)/shard_map/all_gather | solution.py:77
  7.9 230.1 %all-gather.6.cloned.1.call-start = ((), (), s32[]{:S(2)}) async-start(), calls=%async_computation.1 | async-start | bytes 2621440 | tf_op jit(solution)/shard_map/all_gather | solution.py:124
  183.1 11.3 %copy-start.2 = (s32[8]{0:T(128)S(1)}, s32[8]{0:T(128)}, u32[]{:S(2)}) copy-start(s32[8]{0:T(128)} %param.13) | copy-start | bytes 100
  193.7 331.4 %all-gather.8.cloned.1.call-start = ((), (), s32[]{:S(2)}) async-start(), calls=%async_computation.2 | async-start | bytes 20971520 | tf_op jit(solution)/shard_map/all_gather | solution.py:76
  591.0 3.5 copy-start
  597.5 1.0 copy-start.1
Sparse Core Ops, SparseCore 0:
  9.6 152.3 all-gather.3
  193.8 44.1 all-gather.5
  239.5 285.4 all-gather.7
where the time goes:
time: 628 us; the launch traced here: 618 us
  waiting for transfers between devices  471 us (75%)
  local copies, waits for them, and re-layouts  82.8 us (13%)
  matrix products  28 us (4%)
  between operations  14.6 us (2%)
  other arithmetic  14 us (2%)
  loops' own time  7.84 us (1%)
    all_gather x1, waiting for transfers between devices, local(): lax.all_gather(w_query, 'seq', axis=0, tiled=True)  280 us
    all_gather x1, waiting for transfers between devices, local(): lax.all_gather(w_keyval, 'seq', axis=0, tiled=True)  150 us
    reshape x1, local copies, waits for them, and re-layouts, local(): whole_query.reshape(features, -1)  41 us
    all_gather x1, waiting for transfers between devices, local(): portion = lax.all_gather(kv_cache, 'seq', axis=0, tiled=True)  40.1 us
    reshape x1, local copies, waits for them, and re-layouts, local(): whole_keyval.reshape(features, -1)  21.2 us
    dot_general x1, matrix products, local(): jnp.dot(hidden, whole_query.reshape(features, -1), preferred_element_type...  14.2 us
  transfers between devices with their start and end apart: 3, of which 3 were waited for; matrix products, arithmetic and copies ran while one was open for 2% of the time, Pallas kernels for 0%

commit v1 on v0

v1 whole, which is shorter than its diff:
```python
import functools
import math

import jax
import jax.numpy as jnp
from jax import lax
from jax.experimental import pallas as pl
from jax.experimental.pallas import tpu as pltpu
from jax.sharding import PartitionSpec as P

CH = 256
MESH = pl.DeviceIdType.MESH

theta_base = 500000.0
lowest = -1e30


def rotary_tables(positions, head_width):
    half_width = head_width // 2
    frequency = theta_base ** (
        -(jnp.arange(half_width, dtype=jnp.float32) * 2.0) / head_width
    )
    angles = positions.astype(jnp.float32)[:, None] * frequency[None, :]
    cosine, sine = jnp.cos(angles), jnp.sin(angles)
    return jnp.concatenate([cosine, cosine], -1), jnp.concatenate([-sine, sine], -1)


def kernel(
    n, groups, local_heads, group_size,
    hidden_hbm, own_w, stored, cos_ref, sin_ref, qpos_ref, done_ref, kpos_ref,
    out_ref, cache_ref,
    hid, wbuf, kvbuf, qbuf, acc,
    hid_sem, own_sem, up_send, down_send, z_recv, y_send, y_recv,
    kv_up, kv_down, kv_recv,
):
    s = lax.axis_index("seq")
    g = lax.axis_index("grp")
    rows = hid.shape[0]
    chunks, depth, width = own_w.shape
    part = depth // groups
    planes = 2 * local_heads
    has_up, has_down = s + 1 < n, s > 0

    barrier = pltpu.get_barrier_semaphore()

    @pl.when(has_up)
    def _():
        pl.semaphore_signal(barrier, inc=1, device_id={"seq": s + 1}, device_id_type=MESH)

    @pl.when(has_down)
    def _():
        pl.semaphore_signal(barrier, inc=1, device_id={"seq": s - 1}, device_id_type=MESH)

    for k in range(1, groups):
        pl.semaphore_signal(
            barrier, inc=1, device_id={"grp": lax.rem(g + k, groups)}, device_id_type=MESH
        )
    hid_copy = pltpu.make_async_copy(hidden_hbm, hid, hid_sem)
    hid_copy.start()
    own_copy = pltpu.make_async_copy(
        own_w, wbuf.at[:, pl.ds(pl.multiple_of(s * depth, depth), depth), :], own_sem
    )
    own_copy.start()
    pl.semaphore_wait(
        barrier, jnp.where(has_up, 1, 0) + jnp.where(has_down, 1, 0) + (groups - 1)
    )

    def piece(c, o, gg):
        return wbuf.at[c, pl.ds(pl.multiple_of(o * depth + gg * part, part), part), :]

    def kv_piece(j, o):
        return kvbuf.at[j, pl.ds(pl.multiple_of(o * rows, rows), rows), :]

    def up_copy(c, o, src):
        return pltpu.make_async_remote_copy(
            src_ref=src, dst_ref=piece(c, o, g), send_sem=up_send.at[c, o],
            recv_sem=z_recv.at[c, o], device_id={"seq": s + 1}, device_id_type=MESH,
        )

    def down_copy(c, o, src):
        return pltpu.make_async_remote_copy(
            src_ref=src, dst_ref=piece(c, o, g), send_sem=down_send.at[c, o],
            recv_sem=z_recv.at[c, o], device_id={"seq": s - 1}, device_id_type=MESH,
        )

    def side_copy(c, o, sender, target):
        return pltpu.make_async_remote_copy(
            src_ref=piece(c, o, sender), dst_ref=piece(c, o, sender),
            send_sem=y_send.at[c, o, target], recv_sem=y_recv.at[c, o, sender],
            device_id={"grp": target}, device_id_type=MESH,
        )

    def kv_up_copy(j, o):
        return pltpu.make_async_remote_copy(
            src_ref=kv_piece(j, o), dst_ref=kv_piece(j, o), send_sem=kv_up.at[j, o],
            recv_sem=kv_recv.at[j, o], device_id={"seq": s + 1}, device_id_type=MESH,
        )

    def kv_down_copy(j, o):
        return pltpu.make_async_remote_copy(
            src_ref=kv_piece(j, o), dst_ref=kv_piece(j, o), send_sem=kv_down.at[j, o],
            recv_sem=kv_recv.at[j, o], device_id={"seq": s - 1}, device_id_type=MESH,
        )

    def send_own(c):
        src = own_w.at[c, pl.ds(pl.multiple_of(g * part, part), part), :]

        @pl.when(has_up)
        def _():
            up_copy(c, s, src).start()

        @pl.when(has_down)
        def _():
            down_copy(c, s, src).start()

    def forward(c):
        def hop(d, _):
            lo, hi = s - d, s + d

            @pl.when(lo >= 0)
            def _():
                up_copy(c, lo, piece(c, lo, g)).wait_recv()

                @pl.when(has_up)
                def _():
                    up_copy(c, lo, piece(c, lo, g)).start()

                for k in range(1, groups):
                    side_copy(c, lo, g, lax.rem(g + k, groups)).start()

            @pl.when(hi < n)
            def _():
                down_copy(c, hi, piece(c, hi, g)).wait_recv()

                @pl.when(has_down)
                def _():
                    down_copy(c, hi, piece(c, hi, g)).start()

                for k in range(1, groups):
                    side_copy(c, hi, g, lax.rem(g + k, groups)).start()

            return 0

        lax.fori_loop(1, n, hop, 0)

    def kv_hop(j, d):
        lo, hi = s - d, s + d

        @pl.when(lo >= 0)
        def _():
            kv_up_copy(j, lo).wait_recv()

            @pl.when(has_up)
            def _():
                kv_up_copy(j, lo).start()

        @pl.when(hi < n)
        def _():
            kv_down_copy(j, hi).wait_recv()

            @pl.when(has_down)
            def _():
                kv_down_copy(j, hi).start()

    def project(c):
        def gather_side(o, _):
            @pl.when(o != s)
            def _():
                for k in range(1, groups):
                    other = lax.rem(g + k, groups)
                    side_copy(c, o, other, g).wait_recv()

            return 0

        lax.fori_loop(0, n, gather_side, 0)
        acc[...] = jnp.zeros_like(acc)

        def add(o, _):
            at = pl.ds(pl.multiple_of(o * depth, depth), depth)
            acc[...] += jnp.dot(
                hid[:, at], wbuf[c, at, :], preferred_element_type=jnp.float32
            )
            return 0

        lax.fori_loop(0, n, add, 0)

    def rotated():
        raw = acc[...]
        half = width // 2
        turned = jnp.concatenate([raw[:, half:], raw[:, :half]], -1)
        return raw * cos_ref[...] + turned * sin_ref[...]

    row_block = 128
    scale = width ** (-0.5) * math.log2(math.e)

    def attend(q):
        head = q // group_size

        def block(b, _):
            at = pl.ds(pl.multiple_of(b * row_block, row_block), row_block)
            scores = lax.dot_general(
                qbuf[at, :], kvbuf[2 * head], (((1,), (1,)), ((), ())),
                preferred_element_type=jnp.float32,
            ) * scale
            scores = jnp.where(kpos_ref[...] <= qpos_ref[at, :], scores, lowest)
            top = scores.max(-1, keepdims=True)
            weights = jnp.exp2(scores - top)
            total = weights.sum(-1, keepdims=True)
            mixed = jnp.dot(
                weights.astype(jnp.bfloat16), kvbuf[2 * head + 1],
                preferred_element_type=jnp.float32,
            ) / total
            out_ref[q, at, :] = jnp.where(done_ref[at, :] > 0, mixed, 0.0).astype(jnp.bfloat16)
            return 0

        lax.fori_loop(0, rows // row_block, block, 0)

    send_own(0)

    @pl.when(chunks > 1)
    def _():
        send_own(1)

    own_copy.wait()
    hid_copy.wait()

    def turn(t, _):
        @pl.when(t + 2 < chunks)
        def _():
            send_own(t + 2)

        @pl.when(t < chunks)
        def _():
            forward(t)

        for j in range(planes):
            last = planes + (j // 2) * group_size + 1

            @pl.when((t - 1 - j >= 1) & (t - 1 - j < n) & (t <= last))
            def _(j=j):
                kv_hop(j, t - 1 - j)

            @pl.when(t == last)
            def _(j=j):
                def rest(d, _):
                    kv_hop(j, d)
                    return 0

                lax.fori_loop(last - j, n, rest, 0)

        c = t - 1

        @pl.when(t >= 1)
        def _():
            project(c)

        @pl.when((t >= 1) & (c < planes))
        def _():
            fresh = jnp.where(lax.rem(c, 2) == 0, rotated(), acc[...]).astype(jnp.bfloat16)
            fresh = jnp.where(done_ref[...] > 0, fresh, stored[c])
            cache_ref[c] = fresh
            kvbuf[c, pl.ds(pl.multiple_of(s * rows, rows), rows), :] = fresh

            @pl.when(has_up)
            def _():
                kv_up_copy(c, s).start()

            @pl.when(has_down)
            def _():
                kv_down_copy(c, s).start()

        @pl.when(c >= planes)
        def _():
            qbuf[...] = rotated().astype(jnp.bfloat16)
            attend(c - planes)

        return 0

    lax.fori_loop(0, chunks + 1, turn, 0)

    def drain(c, _):
        def each(o, _):
            @pl.when(has_up & (o <= s))
            def _():
                up_copy(c, o, piece(c, o, g)).wait_send()

            @pl.when(has_down & (o >= s))
            def _():
                down_copy(c, o, piece(c, o, g)).wait_send()

            @pl.when(o != s)
            def _():
                for k in range(1, groups):
                    side_copy(c, o, g, lax.rem(g + k, groups)).wait_send()

            return 0

        lax.fori_loop(0, n, each, 0)
        return 0

    lax.fori_loop(0, chunks, drain, 0)

    def kv_drain(j, _):
        def each(o, _):
            @pl.when(has_up & (o <= s))
            def _():
                kv_up_copy(j, o).wait_send()

            @pl.when(has_down & (o >= s))
            def _():
                kv_down_copy(j, o).wait_send()

            return 0

        lax.fori_loop(0, n, each, 0)
        return 0

    lax.fori_loop(0, planes, kv_drain, 0)


def local(n, groups, meet_span, span_map, hidden, w_query, w_keyval, stored_kv):
    row_count, features = hidden.shape
    span_count = span_map.shape[0]
    depth, local_heads = w_query.shape[:2]
    head_width = stored_kv.shape[2] // 2
    group_size = w_query.shape[2] // head_width
    span_len = CH
    slots_dev = row_count // span_len
    planes, heads = 2 * local_heads, local_heads * group_size
    chunks = planes + heads
    offsets = jnp.arange(span_len, dtype=jnp.int32)
    key_pos = (span_map[:, None] * span_len + offsets[None, :]).reshape(1, -1)
    seq_index = lax.axis_index("seq")
    my_spans = lax.dynamic_slice_in_dim(span_map, seq_index * slots_dev, slots_dev, 0)
    positions = (my_spans[:, None] * span_len + offsets[None, :]).reshape(-1)
    computed_slot = (my_spans < meet_span[0]) | (my_spans == span_count - 1)
    done = jnp.repeat(computed_slot, span_len).astype(jnp.int32)[:, None]
    cosine, sine = rotary_tables(positions, head_width)
    own_w = jnp.concatenate(
        [
            w_keyval.reshape(depth, planes, head_width),
            w_query.reshape(depth, heads, head_width),
        ],
        1,
    ).transpose(1, 0, 2)
    stored = stored_kv.reshape(row_count, planes, head_width).transpose(1, 0, 2)
    vmem = pl.BlockSpec(memory_space=pltpu.VMEM)
    hbm = pl.BlockSpec(memory_space=pl.ANY)
    dma = pltpu.SemaphoreType.DMA
    attended, cache = pl.pallas_call(
        functools.partial(kernel, n, groups, local_heads, group_size),
        out_shape=(
            jax.ShapeDtypeStruct((heads, row_count, head_width), jnp.bfloat16),
            jax.ShapeDtypeStruct((planes, row_count, head_width), jnp.bfloat16),
        ),
        in_specs=[hbm, hbm, vmem, vmem, vmem, vmem, vmem, vmem],
        out_specs=(vmem, vmem),
        scratch_shapes=[
            pltpu.VMEM((row_count, features), jnp.bfloat16),
            pltpu.VMEM((chunks, features, head_width), jnp.bfloat16),
            pltpu.VMEM((planes, n * row_count, head_width), jnp.bfloat16),
            pltpu.VMEM((row_count, head_width), jnp.bfloat16),
            pltpu.VMEM((row_count, head_width), jnp.float32),
            dma,
            dma,
            dma((chunks, n)),
            dma((chunks, n)),
            dma((chunks, n)),
            dma((chunks, n, groups)),
            dma((chunks, n, groups)),
            dma((planes, n)),
            dma((planes, n)),
            dma((planes, n)),
        ],
        compiler_params=pltpu.CompilerParams(
            collective_id=0, has_side_effects=True, vmem_limit_bytes=58 * 1024 * 1024
        ),
    )(hidden, own_w, stored, cosine, sine, positions[:, None], done, key_pos)
    attended = attended.transpose(1, 0, 2).reshape(row_count, local_heads, -1)
    cache = cache.transpose(1, 0, 2).reshape(row_count, local_heads, -1)
    return (attended, cache)


def solution(mesh):
    return jax.shard_map(
        functools.partial(local, mesh.shape["seq"], mesh.shape["grp"]),
        mesh=mesh,
        in_specs=(
            P("grp"),
            P("grp"),
            P(("grp", "seq"), None),
            P("seq", ("head", "hold"), None),
            P("seq", ("head", "hold"), None),
            P(("grp", "seq"), ("head", "hold"), None),
        ),
        out_specs=(
            P(("grp", "seq"), ("head", "hold"), None),
            P(("grp", "seq"), ("head", "hold"), None),
        ),
        check_vma=False,
    )
```

time: 628 us -> 319 us (0.51); the launches traced: 618 us -> 319 us
  waiting for transfers between devices: 471 us -> 0 us
  Pallas kernels: 0 us -> 275 us
  local copies, waits for them, and re-layouts: 82.8 us -> 34.1 us
  matrix products: 28 us -> 0 us
  between operations: 14.6 us -> 1.35 us
  loops' own time: 7.84 us -> 0 us
    all_gather x3 -> x0, waiting for transfers between devices: 470 us -> none  [the longest x1 280 us: local(): lax.all_gather(w_query, 'seq', axis=0, tiled=True)]
    pallas_call x0 -> x1, Pallas kernels: none -> 275 us  [local(): pl.pallas_call(functools.partial(kernel, n, groups, local_heads, group_si...]
    reshape x5 -> x3, local copies, waits for them, and re-layouts: 65.9 us -> 9.97 us  [the longest x1 6.46 us: local(): w_query.reshape(depth, heads, head_width)]
    dot_general x4 -> x0, matrix products: 28 us -> none  [the longest x1 14.2 us: local(): jnp.dot(hidden, whole_query.reshape(features, -1), preferred_element_type...]
    unnamed x6 -> x18, local copies, waits for them, and re-layouts: 7.39 us -> 22.3 us
    another operation x5 -> x0, loops' own time: 7.84 us -> none  [the longest x1 7.71 us: local(): fold_result, _ = lax.scan(scan_step, start_state, (blocked, blocked_pos))]
  transfers between devices with their start and end apart: 3 -> 0, of which waited for: 3 -> 0; matrix products, arithmetic and copies ran while one was open for 2% -> 0% of each run, Pallas kernels for 0% -> 0%
where the time goes in v1:
time: 319 us
  Pallas kernels  275 us (86%)
  local copies, waits for them, and re-layouts  34.1 us (11%)
  other arithmetic  8.43 us (3%)
    pallas_call x1, Pallas kernels, local(): pl.pallas_call(functools.partial(kernel, n, groups, local_heads, group_si...  275 us
    unnamed x18, local copies, waits for them, and re-layouts  22.3 us
    reshape x1, local copies, waits for them, and re-layouts, local(): w_query.reshape(depth, heads, head_width)  6.46 us

profile of v1, /device:TPU:0, one launch (start us, length us, event | category | flops | bytes accessed | tf_op | source)
XLA Modules:
  0.0 318.7 jit_solution(12811136971367040181)
XLA Ops:
  0.6 11.2 %copy.9 = bf16[2048,2,512]{0,2,1:T(8,128)(2,1)} copy(bf16[2048,2,512]{2,1,0:T(2,128)(2,1)} %param.9) | data formatting | bytes 8388608 | tf_op args[3]
  11.8 6.5 %copy.11 = bf16[2048,8,128]{2,0,1:T(8,128)(2,1)} copy(bf16[2048,8,128]{0,2,1:T(8,128)(2,1)} %bitcast.29) | data formatting | bytes 8388608 | tf_op jit(solution)/shard_map/reshape | solution.py:342
  18.2 4.7 %copy.8 = bf16[2048,2,256]{0,2,1:T(8,128)(2,1)S(1)} copy(bf16[2048,2,256]{2,1,0:T(2,128)(2,1)} %param.10) | data formatting | bytes 4194304 | tf_op args[4]
  23.0 2.5 copy.10
  25.5 0.0 copy-start
  25.5 0.0 copy-start.2
  25.5 6.1 %maximum_bitcast_fusion.own_w = bf16[12,2048,128]{2,1,0:T(8,128)(2,1)} fusion(bf16[2048,8,128]{2,0,1:T(8,128)(2,1)} %copy.11, bf16[2048,4,128]{2,0,1:T(8,128)(2,1)} %copy.10), kind=kLoop, calls=%fused_computation | loop fusion | flops 3145728 | bytes 12582912 | tf_op jit(solution)/shard_map/transpose | solution.py:345
  31.6 0.0 copy-done
  31.6 0.7 copy.12
  32.4 1.0 copy.13
  33.4 0.0 copy-done.2
  33.4 0.1 broadcast_multiply_fusion.1
  33.4 0.1 fusion.1
  33.5 1.0 fusion
  34.5 1.0 pad_maximum_fusion
  35.5 0.9 copy.22
  37.1 0.1 or_convert_fusion
  37.2 0.1 broadcast_bitcast_fusion
  37.3 0.9 copy.24
  38.1 0.1 add_bitcast_fusion
  38.2 0.6 copy.25
  38.8 274.8 %shard_map.77 = (bf16[8,512,128]{2,1,0:T(8,128)(2,1)}, bf16[4,512,128]{2,1,0:T(8,128)(2,1)}) custom-call(bf16[512,8192]{1,0:T(8,128)(2,1)} %hidden_hbm.1, bf16[12,2048,128]{2,1,0:T(8,128)(2,1)} %maximum_bitcast_fusion.own_w, bf16[4,512,128]{2,1,0:T(8,128)(2,1)} %bitcast.32, f32[512,128]{1,0:T(8,128)} %get-tuple-element.13.cos_ref, ...), custom_call_target="tpu_custom_call" | custom-call | tf_op jit(solution)/shard_map/pallas_call | solution.py:350
  313.7 0.0 copy-start.1
  313.7 1.5 copy.16
  315.2 2.1 copy.18
  317.3 0.0 copy-done.1
  317.3 0.2 copy.17
  317.5 1.1 copy.19
  (5 shorter events, 0.0 us)
Async XLA Ops:
  25.5 6.1 %copy-start = (bf16[512,2,256]{2,1,0:T(2,128)(2,1)S(1)}, bf16[512,2,256]{2,1,0:T(2,128)(2,1)}, u32[]{:S(2)}) copy-start(bf16[512,2,256]{2,1,0:T(2,128)(2,1)} %param.11) | copy-start | bytes 1572868
  25.5 7.9 %copy-start.2 = (s32[8]{0:T(128)S(1)}, s32[8]{0:T(128)}, u32[]{:S(2)}) copy-start(s32[8]{0:T(128)} %param.7) | copy-start | bytes 100
  313.7 3.7 %copy-start.1 = (bf16[4,512,128]{2,1,0:T(8,128)(2,1)S(1)}, bf16[4,512,128]{2,1,0:T(8,128)(2,1)}, u32[]{:S(2)}) copy-start(bf16[4,512,128]{2,1,0:T(8,128)(2,1)} %get-tuple-element.5) | copy-start | bytes 1572868

commit v2 on v1

v2 whole, which is shorter than its diff:
```python
import functools
import math

import jax
import jax.numpy as jnp
from jax import lax
from jax.experimental import pallas as pl
from jax.experimental.pallas import tpu as pltpu
from jax.sharding import PartitionSpec as P

CH = 256
MESH = pl.DeviceIdType.MESH

theta_base = 500000.0
lowest = -1e30


def rotary_tables(positions, head_width):
    half_width = head_width // 2
    frequency = theta_base ** (
        -(jnp.arange(half_width, dtype=jnp.float32) * 2.0) / head_width
    )
    angles = positions.astype(jnp.float32)[:, None] * frequency[None, :]
    cosine, sine = jnp.cos(angles), jnp.sin(angles)
    return jnp.concatenate([cosine, cosine], -1), jnp.concatenate([-sine, sine], -1)


def kernel(
    n, groups, head_dev, hold_dev, local_heads, group_size,
    hidden_hbm, own_kv, own_q, stored_hbm, cos_ref, sin_ref, qpos_ref, done_ref, kpos_ref,
    out_ref, cache_ref,
    hid, wbuf, kvbuf, stored, gout, qbuf, acc,
    hid_sem, st_sem, own_sem, up_send, down_send, z_recv, y_send, y_recv,
    kv_up, kv_down, kv_recv,
    lend_send, lend_recv, x_send, x_recv, mate_send, mate_recv,
    st_send, st_recv, back_send, back_recv, ret_send, ret_recv,
):
    s = lax.axis_index("seq")
    g = lax.axis_index("grp")
    hx = lax.axis_index("head")
    hc = lax.axis_index("hold")
    planes, rows, width = cache_ref.shape
    heads = out_ref.shape[0]
    chunks = planes + heads
    depth = own_kv.shape[0]
    part = depth if groups == 1 else (depth // 16) * 9
    rest_part = depth - part
    subs = lend_send.shape[0]
    sub_width = hid.shape[1] // subs
    lent_rows = rows // (head_dev * hold_dev)
    idle = (s == 0) | (s == n - 1)
    host = (s == 1) | (s == n - 2)
    partner = jnp.where(s == 0, 1, n - 2)
    guest = jnp.where(s == 1, 0, n - 1)
    has_up, has_down = (s < n - 2) & ~idle, (s > 1) & ~idle
    near_up, near_down = s + 1 < n, s > 0
    row_groups = jnp.where(idle, 0, jnp.where(host, 2, 1))

    barrier = pltpu.get_barrier_semaphore()

    def greet(device):
        pl.semaphore_signal(barrier, inc=1, device_id=device, device_id_type=MESH)

    @pl.when(near_up)
    def _():
        greet({"seq": s + 1})

    @pl.when(near_down)
    def _():
        greet({"seq": s - 1})

    for k in range(1, groups):
        greet({"grp": lax.rem(g + k, groups)})
    for k in range(1, head_dev):
        greet({"head": lax.rem(hx + k, head_dev)})
    for k in range(1, hold_dev):
        greet({"hold": lax.rem(hc + k, hold_dev)})

    def columns(c):
        return pl.ds(pl.multiple_of(c * width, width), width)

    def row_range(i):
        return pl.ds(pl.multiple_of(i * rows, rows), rows)

    hid_copy = pltpu.make_async_copy(hidden_hbm, hid.at[pl.ds(0, rows), :], hid_sem)
    hid_copy.start()
    st_copy = pltpu.make_async_copy(stored_hbm, stored.at[:, pl.ds(0, rows), :], st_sem)
    st_copy.start()

    def own_copy(c):
        own = own_kv.at[:, columns(c)] if c < planes else own_q.at[:, columns(c - planes)]
        return pltpu.make_async_copy(
            own, wbuf.at[c, pl.ds(pl.multiple_of(s * depth, depth), depth), :], own_sem.at[c]
        )

    for c in range(chunks):
        own_copy(c).start()
    pl.semaphore_wait(
        barrier,
        jnp.where(near_up, 1, 0) + jnp.where(near_down, 1, 0)
        + (groups - 1 + head_dev - 1 + hold_dev - 1),
    )

    def piece(c, o):
        return wbuf.at[c, pl.ds(pl.multiple_of(o * depth + g * rest_part, 16), part), :]

    def side_piece(c, o, sender):
        return wbuf.at[c, pl.ds(pl.multiple_of(o * depth + sender * part, 16), rest_part), :]

    def kv_piece(j, o):
        return kvbuf.at[j, row_range(o), :]

    def remote(src, dst, send_sem, recv_sem, **device):
        return pltpu.make_async_remote_copy(
            src_ref=src, dst_ref=dst, send_sem=send_sem, recv_sem=recv_sem,
            device_id=device, device_id_type=MESH,
        )

    def up_copy(c, o, src=None):
        src = piece(c, o) if src is None else src
        return remote(src, piece(c, o), up_send.at[c, o], z_recv.at[c, o], seq=s + 1)

    def down_copy(c, o, src=None):
        src = piece(c, o) if src is None else src
        return remote(src, piece(c, o), down_send.at[c, o], z_recv.at[c, o], seq=s - 1)

    def side_copy(c, o, sender, target):
        at = side_piece(c, o, sender)
        return remote(at, at, y_send.at[c, o], y_recv.at[c, o], grp=target)

    def kv_up_copy(j, o):
        at = kv_piece(j, o)
        return remote(at, at, kv_up.at[j, o], kv_recv.at[j, o], seq=s + 1)

    def kv_down_copy(j, o):
        at = kv_piece(j, o)
        return remote(at, at, kv_down.at[j, o], kv_recv.at[j, o], seq=s - 1)

    def hid_piece(x, h, k):
        start = rows + (x * hold_dev + h) * lent_rows
        return hid.at[
            pl.ds(pl.multiple_of(start, 16), lent_rows), pl.ds(k * sub_width, sub_width)
        ]

    def lend_copy(k):
        start = (hx * hold_dev + hc) * lent_rows
        src = hidden_hbm.at[
            pl.ds(pl.multiple_of(start, 16), lent_rows), pl.ds(k * sub_width, sub_width)
        ]
        return remote(src, hid_piece(hx, hc, k), lend_send.at[k], lend_recv.at[k], seq=partner)

    def x_copy(k, x, target):
        at = hid_piece(x, hc, k)
        return remote(at, at, x_send.at[k, target], x_recv.at[k, x], head=target)

    def mate_copy(k, x, h, target):
        at = hid_piece(x, h, k)
        return remote(at, at, mate_send.at[k, x, target], mate_recv.at[k, x, h], hold=target)

    def st_lend():
        return remote(
            stored_hbm, stored.at[:, pl.ds(rows, rows), :], st_send, st_recv, seq=partner
        )

    def back_copy(j):
        return remote(
            kv_piece(j, guest), cache_ref.at[j], back_send.at[j], back_recv.at[j], seq=guest
        )

    def ret_copy(q):
        return remote(gout.at[q], out_ref.at[q], ret_send.at[q], ret_recv.at[q], seq=guest)

    def send_own(c):
        at = pl.ds(pl.multiple_of(g * rest_part, 16), part)
        src = own_kv.at[at, columns(c)] if c < planes else own_q.at[at, columns(c - planes)]

        @pl.when(has_up)
        def _():
            up_copy(c, s, src).start()

        @pl.when(has_down)
        def _():
            down_copy(c, s, src).start()

    def spread(c, o):
        for k in range(1, groups):
            side_copy(c, o, g, lax.rem(g + k, groups)).start()

    def forward(c):
        def hop(d, _):
            lo, hi = s - d, s + d

            @pl.when((lo >= 0) & ~idle)
            def _():
                up_copy(c, lo).wait_recv()

                @pl.when(has_up)
                def _():
                    up_copy(c, lo).start()

                spread(c, lo)

            @pl.when((hi < n) & ~idle)
            def _():
                down_copy(c, hi).wait_recv()

                @pl.when(has_down)
                def _():
                    down_copy(c, hi).start()

                spread(c, hi)

            return 0

        lax.fori_loop(1, n, hop, 0)

    def kv_hop(j, d):
        lo, hi = s - d, s + d

        @pl.when((lo >= 0) & (s > 1) & ~idle)
        def _():
            kv_up_copy(j, lo).wait_recv()

            @pl.when(has_up)
            def _():
                kv_up_copy(j, lo).start()

        @pl.when((hi < n) & (s < n - 2) & ~idle)
        def _():
            kv_down_copy(j, hi).wait_recv()

            @pl.when(has_down)
            def _():
                kv_down_copy(j, hi).start()

    def gather_side(c):
        def each(o, _):
            @pl.when((o != s) & ~idle)
            def _():
                for k in range(1, groups):
                    side_copy(c, o, lax.rem(g + k, groups), g).wait_recv()

            return 0

        lax.fori_loop(0, n, each, 0)

    def project(c, r):
        acc[...] = jnp.zeros_like(acc)

        def add(o, _):
            at = pl.ds(pl.multiple_of(o * depth, depth), depth)
            acc[...] += jnp.dot(
                hid[row_range(r), at], wbuf[c, at, :], preferred_element_type=jnp.float32
            )
            return 0

        lax.fori_loop(0, n, add, 0)

    def rotated(r):
        raw = acc[...]
        half = width // 2
        turned = jnp.concatenate([raw[:, half:], raw[:, :half]], -1)
        return raw * cos_ref[row_range(r), :] + turned * sin_ref[row_range(r), :]

    def make_plane(c, r):
        project(c, r)
        fresh = jnp.where(lax.rem(c, 2) == 0, rotated(r), acc[...]).astype(jnp.bfloat16)
        fresh = jnp.where(done_ref[row_range(r), :] > 0, fresh, stored[c, row_range(r), :])
        o = jnp.where(r == 0, s, guest)
        kvbuf[c, row_range(o), :] = fresh

        @pl.when(r == 0)
        def _():
            cache_ref[c] = fresh

        @pl.when(r == 1)
        def _():
            back_copy(c).start()

        @pl.when(has_up)
        def _():
            kv_up_copy(c, o).start()

        @pl.when(has_down)
        def _():
            kv_down_copy(c, o).start()

    row_block = 128
    scale = width ** (-0.5) * math.log2(math.e)

    def attend(q, r):
        head = q // group_size

        def block(b, _):
            at = pl.ds(pl.multiple_of(b * row_block, row_block), row_block)
            full = pl.ds(pl.multiple_of(r * rows + b * row_block, row_block), row_block)
            scores = lax.dot_general(
                qbuf[at, :], kvbuf[2 * head], (((1,), (1,)), ((), ())),
                preferred_element_type=jnp.float32,
            ) * scale
            scores = jnp.where(kpos_ref[...] <= qpos_ref[full, :], scores, lowest)
            top = scores.max(-1, keepdims=True)
            weights = jnp.exp2(scores - top)
            total = weights.sum(-1, keepdims=True)
            mixed = jnp.dot(
                weights.astype(jnp.bfloat16), kvbuf[2 * head + 1],
                preferred_element_type=jnp.float32,
            ) / total
            mixed = jnp.where(done_ref[full, :] > 0, mixed, 0.0).astype(jnp.bfloat16)

            @pl.when(r == 0)
            def _():
                out_ref[q, at, :] = mixed

            @pl.when(r == 1)
            def _():
                gout[q, at, :] = mixed

            return 0

        lax.fori_loop(0, rows // row_block, block, 0)

        @pl.when(r == 1)
        def _():
            ret_copy(q).start()

    for c in range(planes):
        send_own(c)

    @pl.when(idle)
    def _():
        def own_to_partner(c):
            at = pl.ds(pl.multiple_of(g * rest_part, 16), part)
            src = own_kv.at[at, columns(c)] if c < planes else own_q.at[at, columns(c - planes)]

            @pl.when(s == 0)
            def _():
                up_copy(c, s, src).start()

            @pl.when(s == n - 1)
            def _():
                down_copy(c, s, src).start()

        for c in range(chunks):
            if c == planes:
                for k in range(subs):
                    lend_copy(k).start()
                st_lend().start()
            own_to_partner(c)

    for c in range(chunks):
        own_copy(c).wait()
    hid_copy.wait()
    st_copy.wait()

    def early(t, _):
        @pl.when(t < planes)
        def _():
            forward(t)

        @pl.when(t == planes - 1)
        def _():
            for c in range(planes, chunks):
                send_own(c)

        @pl.when(t >= 1)
        def _():
            gather_side(t - 1)

            @pl.when(~idle)
            def _():
                make_plane(t - 1, 0)

        return 0

    lax.fori_loop(0, planes + 1, early, 0)

    @pl.when(host)
    def _():
        for k in range(subs):
            lend_copy_in = remote(
                hid_piece(hx, hc, k), hid_piece(hx, hc, k),
                lend_send.at[k], lend_recv.at[k], seq=guest,
            )
            lend_copy_in.wait_recv()
            for i in range(1, head_dev):
                x_copy(k, hx, lax.rem(hx + i, head_dev)).start()
            for i in range(1, hold_dev):
                mate_copy(k, hx, hc, lax.rem(hc + i, hold_dev)).start()
        for k in range(subs):
            for i in range(1, head_dev):
                x = lax.rem(hx + i, head_dev)
                x_copy(k, x, hx).wait_recv()
                for m in range(1, hold_dev):
                    mate_copy(k, x, hc, lax.rem(hc + m, hold_dev)).start()
        for k in range(subs):
            for x in range(head_dev):
                for m in range(1, hold_dev):
                    mate_copy(k, x, lax.rem(hc + m, hold_dev), hc).wait_recv()
        st_in = stored.at[:, pl.ds(rows, rows), :]
        remote(st_in, st_in, st_send, st_recv, seq=guest).wait_recv()

        def guest_plane(c, _):
            make_plane(c, 1)
            return 0

        lax.fori_loop(0, planes, guest_plane, 0)

    def late(t, _):
        @pl.when(t < chunks)
        def _():
            forward(t)

        c = t - 1

        @pl.when(c >= planes)
        def _():
            gather_side(c)
            q = c - planes

            @pl.when(lax.rem(q, group_size) == 0)
            def _():
                def rest(d, _):
                    kv_hop(2 * (q // group_size), d)
                    kv_hop(2 * (q // group_size) + 1, d)
                    return 0

                lax.fori_loop(1, n, rest, 0)

            def each(r, _):
                project(c, r)
                qbuf[...] = rotated(r).astype(jnp.bfloat16)
                attend(q, r)
                return 0

            lax.fori_loop(0, row_groups, each, 0)

        return 0

    lax.fori_loop(planes, chunks + 1, late, 0)

    def drain(c, _):
        def each(o, _):
            @pl.when((has_up & (o <= s)) | ((s == 0) & (o == 0)))
            def _():
                up_copy(c, o).wait_send()

            @pl.when((has_down & (o >= s)) | ((s == n - 1) & (o == n - 1)))
            def _():
                down_copy(c, o).wait_send()

            @pl.when((o != s) & ~idle)
            def _():
                for k in range(1, groups):
                    side_copy(c, o, g, lax.rem(g + k, groups)).wait_send()

            return 0

        lax.fori_loop(0, n, each, 0)
        return 0

    lax.fori_loop(0, chunks, drain, 0)

    def kv_drain(j, _):
        def each(o, _):
            @pl.when(has_up & (o <= s))
            def _():
                kv_up_copy(j, o).wait_send()

            @pl.when(has_down & (o >= s))
            def _():
                kv_down_copy(j, o).wait_send()

            return 0

        lax.fori_loop(0, n, each, 0)

        @pl.when(host)
        def _():
            back_copy(j).wait_send()

        @pl.when(idle)
        def _():
            at = cache_ref.at[j]
            remote(at, at, back_send.at[j], back_recv.at[j], seq=partner).wait_recv()

        return 0

    lax.fori_loop(0, planes, kv_drain, 0)

    @pl.when(host)
    def _():
        for k in range(subs):
            for i in range(1, head_dev):
                x_copy(k, hx, lax.rem(hx + i, head_dev)).wait_send()
            for x in range(head_dev):
                for m in range(1, hold_dev):
                    mate_copy(k, x, hc, lax.rem(hc + m, hold_dev)).wait_send()
        for q in range(heads):
            ret_copy(q).wait_send()

    @pl.when(idle)
    def _():
        for k in range(subs):
            lend_copy(k).wait_send()
        st_lend().wait_send()
        for q in range(heads):
            at = out_ref.at[q]
            remote(at, at, ret_send.at[q], ret_recv.at[q], seq=partner).wait_recv()


def local(n, groups, head_dev, hold_dev, meet_span, span_map, hidden, w_query, w_keyval, stored_kv):
    row_count, features = hidden.shape
    span_count = span_map.shape[0]
    depth, local_heads = w_query.shape[:2]
    head_width = stored_kv.shape[2] // 2
    group_size = w_query.shape[2] // head_width
    span_len = CH
    slots_dev = row_count // span_len
    planes, heads = 2 * local_heads, local_heads * group_size
    chunks = planes + heads
    offsets = jnp.arange(span_len, dtype=jnp.int32)
    key_pos = (span_map[:, None] * span_len + offsets[None, :]).reshape(1, -1)
    seq_index = lax.axis_index("seq")
    guest = jnp.where(seq_index == 1, 0, n - 1)
    my_spans = jnp.concatenate(
        [
            lax.dynamic_slice_in_dim(span_map, index * slots_dev, slots_dev, 0)
            for index in (seq_index, guest)
        ]
    )
    positions = (my_spans[:, None] * span_len + offsets[None, :]).reshape(-1)
    computed_slot = (my_spans < meet_span[0]) | (my_spans == span_count - 1)
    done = jnp.repeat(computed_slot, span_len).astype(jnp.int32)[:, None]
    cosine, sine = rotary_tables(positions, head_width)
    own_kv = w_keyval.reshape(depth, planes * head_width)
    own_q = w_query.reshape(depth, heads * head_width)
    stored = stored_kv.reshape(row_count, planes, head_width).transpose(1, 0, 2)
    subs = 4
    vmem = pl.BlockSpec(memory_space=pltpu.VMEM)
    hbm = pl.BlockSpec(memory_space=pl.ANY)
    dma = pltpu.SemaphoreType.DMA
    attended, cache = pl.pallas_call(
        functools.partial(kernel, n, groups, head_dev, hold_dev, local_heads, group_size),
        out_shape=(
            jax.ShapeDtypeStruct((heads, row_count, head_width), jnp.bfloat16),
            jax.ShapeDtypeStruct((planes, row_count, head_width), jnp.bfloat16),
        ),
        in_specs=[hbm] * 4 + [vmem] * 5,
        out_specs=(vmem, vmem),
        scratch_shapes=[
            pltpu.VMEM((2 * row_count, features), jnp.bfloat16),
            pltpu.VMEM((chunks, features, head_width), jnp.bfloat16),
            pltpu.VMEM((planes, n * row_count, head_width), jnp.bfloat16),
            pltpu.VMEM((planes, 2 * row_count, head_width), jnp.bfloat16),
            pltpu.VMEM((heads, row_count, head_width), jnp.bfloat16),
            pltpu.VMEM((row_count, head_width), jnp.bfloat16),
            pltpu.VMEM((row_count, head_width), jnp.float32),
            dma,
            dma,
            dma((chunks,)),
        ]
        + [dma((chunks, n))] * 5
        + [dma((planes, n))] * 3
        + [dma((subs,))] * 2
        + [dma((subs, head_dev))] * 2
        + [dma((subs, head_dev, hold_dev))] * 2
        + [dma] * 2
        + [dma((planes,))] * 2
        + [dma((heads,))] * 2,
        compiler_params=pltpu.CompilerParams(
            collective_id=0, has_side_effects=True, vmem_limit_bytes=60 * 1024 * 1024
        ),
    )(hidden, own_kv, own_q, stored, cosine, sine, positions[:, None], done, key_pos)
    attended = attended.transpose(1, 0, 2).reshape(row_count, local_heads, -1)
    cache = cache.transpose(1, 0, 2).reshape(row_count, local_heads, -1)
    return (attended, cache)


def solution(mesh):
    return jax.shard_map(
        functools.partial(local, *(mesh.shape[a] for a in ("seq", "grp", "head", "hold"))),
        mesh=mesh,
        in_specs=(
            P("grp"),
            P("grp"),
            P(("grp", "seq"), None),
            P("seq", ("head", "hold"), None),
            P("seq", ("head", "hold"), None),
            P(("grp", "seq"), ("head", "hold"), None),
        ),
        out_specs=(
            P(("grp", "seq"), ("head", "hold"), None),
            P(("grp", "seq"), ("head", "hold"), None),
        ),
        check_vma=False,
    )
```

time: 319 us -> 338 us (1.060)
  Pallas kernels: 275 us -> 317 us
  local copies, waits for them, and re-layouts: 34.1 us -> 15.8 us
  other arithmetic: 8.43 us -> 4.16 us
    pallas_call x1, Pallas kernels: 275 us -> 317 us  [local(): pl.pallas_call(functools.partial(kernel, n, groups, head_dev, hold_dev, l...]
    unnamed x18, local copies, waits for them, and re-layouts: 22.3 us -> 12.3 us
    reshape x2 -> x0, local copies, waits for them, and re-layouts: 8.97 us -> none  [the longest x1 6.46 us: local(): w_query.reshape(depth, heads, head_width)]
    transpose x1 -> x0, other arithmetic: 6.11 us -> none  [local(): own_w = jnp.concatenate([w_keyval.reshape(depth, planes, head_width), w_q...]
where the time goes in v2:
time: 338 us
  Pallas kernels  317 us (94%)
  local copies, waits for them, and re-layouts  15.8 us (5%)
  other arithmetic  4.16 us (1%)
    pallas_call x1, Pallas kernels, local(): pl.pallas_call(functools.partial(kernel, n, groups, head_dev, hold_dev, l...  317 us
    unnamed x18, local copies, waits for them, and re-layouts  12.3 us

profile of v2, /device:TPU:0, one launch (start us, length us, event | category | flops | bytes accessed | tf_op | source)
XLA Modules:
  0.0 338.0 jit_solution(6689922971821244783)
XLA Ops:
  0.6 0.0 copy-start.1
  1.4 0.8 fusion.2
  2.3 0.1 or_convert_fusion
  2.3 0.1 broadcast_multiply_fusion.1
  2.4 0.7 broadcast_multiply_fusion
  3.1 0.1 broadcast_bitcast_fusion
  3.2 0.1 add_bitcast_fusion
  3.2 0.6 copy.23
  3.8 0.1 fusion.1
  3.9 1.1 copy.20
  5.0 1.1 copy.22
  6.1 1.3 copy.8
  7.4 1.0 copy.9
  8.4 0.0 copy-start
  8.4 1.9 fusion
  10.3 1.3 pad_maximum_fusion
  11.6 0.0 copy-done.1
  11.6 1.8 copy.16
  13.4 0.0 copy-done
  13.4 3.1 copy.17
  16.5 316.5 %shard_map.77 = (bf16[8,512,128]{2,1,0:T(8,128)(2,1)}, bf16[4,512,128]{2,1,0:T(8,128)(2,1)}) custom-call(bf16[512,8192]{1,0:T(8,128)(2,1)} %hidden_hbm.1, bf16[2048,512]{1,0:T(8,128)(2,1)} %bitcast.30, bf16[2048,1024]{1,0:T(8,128)(2,1)} %bitcast.29, bf16[4,512,128]{2,1,0:T(8,128)(2,1)} %bitcast.35, f32[1024,128]{1,0:T(8,128)} %get-tuple-element.15.cos_ref, ...), custom_call_target="tpu_custom_call" | custom-call | tf_op jit(solution)/shard_map/pallas_call | solution.py:543
  333.0 0.0 copy-start.2
  333.0 1.5 copy.12
  334.6 2.1 copy.14
  336.7 0.0 copy-done.2
  336.7 0.2 copy.13
  336.9 1.1 copy.15
  (4 shorter events, 0.0 us)
Async XLA Ops:
  0.6 10.9 %copy-start.1 = (bf16[2048,2,256]{2,1,0:T(2,128)(2,1)S(1)}, bf16[2048,2,256]{2,1,0:T(2,128)(2,1)}, u32[]{:S(2)}) copy-start(bf16[2048,2,256]{2,1,0:T(2,128)(2,1)} %param.10) | copy-start | bytes 6291460
  8.4 5.0 %copy-start = (bf16[2048,2,512]{2,1,0:T(2,128)(2,1)S(1)}, bf16[2048,2,512]{2,1,0:T(2,128)(2,1)}, u32[]{:S(2)}) copy-start(bf16[2048,2,512]{2,1,0:T(2,128)(2,1)} %param.9) | copy-start | bytes 12582916
  333.0 3.7 %copy-start.2 = (bf16[4,512,128]{2,1,0:T(8,128)(2,1)S(1)}, bf16[4,512,128]{2,1,0:T(8,128)(2,1)}, u32[]{:S(2)}) copy-start(bf16[4,512,128]{2,1,0:T(8,128)(2,1)} %get-tuple-element.5) | copy-start | bytes 1572868

commit v3 on v2

--- a/solution.py
+++ b/solution.py
@@ -27,9 +27,9 @@
 
 def kernel(
     n, groups, head_dev, hold_dev, local_heads, group_size,
-    hidden_hbm, own_kv, own_q, stored_hbm, cos_ref, sin_ref, qpos_ref, done_ref, kpos_ref,
+    hidden_hbm, own_kv, own_q, stored_hbm, cos_ref, sin_ref, qpos_ref, done_ref, done_row, kpos_ref,
     out_ref, cache_ref,
-    hid, wbuf, kvbuf, stored, gout, qbuf, acc,
+    hid, wbuf, kvbuf, stored, gout, turned_values, acc,
     hid_sem, st_sem, own_sem, up_send, down_send, z_recv, y_send, y_recv,
     kv_up, kv_down, kv_recv,
     lend_send, lend_recv, x_send, x_recv, mate_send, mate_recv,
@@ -249,64 +249,72 @@
 
         def add(o, _):
             at = pl.ds(pl.multiple_of(o * depth, depth), depth)
+            pair = jnp.concatenate([wbuf[c, at, :], wbuf[c + 1, at, :]], -1)
             acc[...] += jnp.dot(
-                hid[row_range(r), at], wbuf[c, at, :], preferred_element_type=jnp.float32
+                hid[row_range(r), at], pair, preferred_element_type=jnp.float32
             )
             return 0
 
         lax.fori_loop(0, n, add, 0)
 
-    def rotated(r):
-        raw = acc[...]
+    def rotated(raw, r):
         half = width // 2
         turned = jnp.concatenate([raw[:, half:], raw[:, :half]], -1)
         return raw * cos_ref[row_range(r), :] + turned * sin_ref[row_range(r), :]
 
-    def make_plane(c, r):
-        project(c, r)
-        fresh = jnp.where(lax.rem(c, 2) == 0, rotated(r), acc[...]).astype(jnp.bfloat16)
-        fresh = jnp.where(done_ref[row_range(r), :] > 0, fresh, stored[c, row_range(r), :])
+    def make_planes(h, r):
+        project(2 * h, r)
         o = jnp.where(r == 0, s, guest)
-        kvbuf[c, row_range(o), :] = fresh
-
-        @pl.when(r == 0)
-        def _():
-            cache_ref[c] = fresh
-
-        @pl.when(r == 1)
-        def _():
-            back_copy(c).start()
-
-        @pl.when(has_up)
-        def _():
-            kv_up_copy(c, o).start()
-
-        @pl.when(has_down)
-        def _():
-            kv_down_copy(c, o).start()
-
-    row_block = 128
+        for i in range(2):
+            c = 2 * h + i
+            raw = acc[:, i * width:(i + 1) * width]
+            fresh = (rotated(raw, r) if i == 0 else raw).astype(jnp.bfloat16)
+            fresh = jnp.where(done_ref[row_range(r), :] > 0, fresh, stored[c, row_range(r), :])
+            kvbuf[c, row_range(o), :] = fresh
+
+            @pl.when(r == 0)
+            def _():
+                cache_ref[c] = fresh
+
+            @pl.when(r == 1)
+            def _():
+                back_copy(c).start()
+
+            @pl.when(has_up)
+            def _():
+                kv_up_copy(c, o).start()
+
+            @pl.when(has_down)
+            def _():
+                kv_down_copy(c, o).start()
+
+    row_block = 256
     scale = width ** (-0.5) * math.log2(math.e)
 
-    def attend(q, r):
+    def attend(q, r, i):
         head = q // group_size
 
         def block(b, _):
             at = pl.ds(pl.multiple_of(b * row_block, row_block), row_block)
             full = pl.ds(pl.multiple_of(r * rows + b * row_block, row_block), row_block)
+            raw = acc[at, i * width:(i + 1) * width]
+            half = width // 2
+            turned = jnp.concatenate([raw[:, half:], raw[:, :half]], -1)
+            queries = (raw * cos_ref[full, :] + turned * sin_ref[full, :]).astype(jnp.bfloat16)
             scores = lax.dot_general(
-                qbuf[at, :], kvbuf[2 * head], (((1,), (1,)), ((), ())),
+                kvbuf[2 * head], queries, (((1,), (1,)), ((), ())),
                 preferred_element_type=jnp.float32,
             ) * scale
-            scores = jnp.where(kpos_ref[...] <= qpos_ref[full, :], scores, lowest)
-            top = scores.max(-1, keepdims=True)
+            key_pos = jnp.concatenate([kpos_ref[...]] * (row_block // width), -1)
+            scores = jnp.where(key_pos <= qpos_ref[:, full], scores, lowest)
+            top = scores.max(0, keepdims=True)
             weights = jnp.exp2(scores - top)
-            total = weights.sum(-1, keepdims=True)
+            total = weights.sum(0, keepdims=True)
             mixed = jnp.dot(
-                weights.astype(jnp.bfloat16), kvbuf[2 * head + 1],
+                turned_values[...], weights.astype(jnp.bfloat16),
                 preferred_element_type=jnp.float32,
             ) / total
-            mixed = jnp.where(done_ref[full, :] > 0, mixed, 0.0).astype(jnp.bfloat16)
+            mixed = jnp.where(done_row[:, full] > 0, mixed, 0.0).T.astype(jnp.bfloat16)
 
             @pl.when(r == 0)
             def _():
@@ -354,26 +362,28 @@
     st_copy.wait()
 
     def early(t, _):
-        @pl.when(t < planes)
-        def _():
-            forward(t)
-
-        @pl.when(t == planes - 1)
+        @pl.when(t < local_heads)
+        def _():
+            forward(2 * t)
+            forward(2 * t + 1)
+
+        @pl.when(t == local_heads - 1)
         def _():
             for c in range(planes, chunks):
                 send_own(c)
 
         @pl.when(t >= 1)
         def _():
-            gather_side(t - 1)
+            gather_side(2 * t - 2)
+            gather_side(2 * t - 1)
 
             @pl.when(~idle)
             def _():
-                make_plane(t - 1, 0)
+                make_planes(t - 1, 0)
 
         return 0
 
-    lax.fori_loop(0, planes + 1, early, 0)
+    lax.fori_loop(0, local_heads + 1, early, 0)
 
     @pl.when(host)
     def _():
@@ -400,44 +410,48 @@
         st_in = stored.at[:, pl.ds(rows, rows), :]
         remote(st_in, st_in, st_send, st_recv, seq=guest).wait_recv()
 
-        def guest_plane(c, _):
-            make_plane(c, 1)
+        def guest_planes(h, _):
+            make_planes(h, 1)
             return 0
 
-        lax.fori_loop(0, planes, guest_plane, 0)
+        lax.fori_loop(0, local_heads, guest_planes, 0)
 
     def late(t, _):
-        @pl.when(t < chunks)
-        def _():
-            forward(t)
-
-        c = t - 1
-
-        @pl.when(c >= planes)
-        def _():
+        @pl.when(t < heads // 2)
+        def _():
+            forward(planes + 2 * t)
+            forward(planes + 2 * t + 1)
+
+        @pl.when(t >= 1)
+        def _():
+            q = 2 * (t - 1)
+            c = planes + q
             gather_side(c)
-            q = c - planes
-
-            @pl.when(lax.rem(q, group_size) == 0)
-            def _():
+            gather_side(c + 1)
+
+            @pl.when((lax.rem(q, group_size) == 0) & ~idle)
+            def _():
+                head = q // group_size
+
                 def rest(d, _):
-                    kv_hop(2 * (q // group_size), d)
-                    kv_hop(2 * (q // group_size) + 1, d)
+                    kv_hop(2 * head, d)
+                    kv_hop(2 * head + 1, d)
                     return 0
 
                 lax.fori_loop(1, n, rest, 0)
+                turned_values[...] = kvbuf[2 * head + 1].T
 
             def each(r, _):
                 project(c, r)
-                qbuf[...] = rotated(r).astype(jnp.bfloat16)
-                attend(q, r)
+                attend(q, r, 0)
+                attend(q + 1, r, 1)
                 return 0
 
             lax.fori_loop(0, row_groups, each, 0)
 
         return 0
 
-    lax.fori_loop(planes, chunks + 1, late, 0)
+    lax.fori_loop(0, heads // 2 + 1, late, 0)
 
     def drain(c, _):
         def each(o, _):
@@ -520,7 +534,8 @@
     planes, heads = 2 * local_heads, local_heads * group_size
     chunks = planes + heads
     offsets = jnp.arange(span_len, dtype=jnp.int32)
-    key_pos = (span_map[:, None] * span_len + offsets[None, :]).reshape(1, -1)
+    key_pos = (span_map[:, None] * span_len + offsets[None, :]).reshape(-1, 1)
+    key_pos = jnp.broadcast_to(key_pos, (key_pos.shape[0], head_width))
     seq_index = lax.axis_index("seq")
     guest = jnp.where(seq_index == 1, 0, n - 1)
     my_spans = jnp.concatenate(
@@ -546,7 +561,7 @@
             jax.ShapeDtypeStruct((heads, row_count, head_width), jnp.bfloat16),
             jax.ShapeDtypeStruct((planes, row_count, head_width), jnp.bfloat16),
         ),
-        in_specs=[hbm] * 4 + [vmem] * 5,
+        in_specs=[hbm] * 4 + [vmem] * 6,
         out_specs=(vmem, vmem),
         scratch_shapes=[
             pltpu.VMEM((2 * row_count, features), jnp.bfloat16),
@@ -554,8 +569,8 @@
             pltpu.VMEM((planes, n * row_count, head_width), jnp.bfloat16),
             pltpu.VMEM((planes, 2 * row_count, head_width), jnp.bfloat16),
             pltpu.VMEM((heads, row_count, head_width), jnp.bfloat16),
-            pltpu.VMEM((row_count, head_width), jnp.bfloat16),
-            pltpu.VMEM((row_count, head_width), jnp.float32),
+            pltpu.VMEM((head_width, n * row_count), jnp.bfloat16),
+            pltpu.VMEM((row_count, 2 * head_width), jnp.float32),
             dma,
             dma,
             dma((chunks,)),
@@ -571,7 +586,7 @@
         compiler_params=pltpu.CompilerParams(
             collective_id=0, has_side_effects=True, vmem_limit_bytes=60 * 1024 * 1024
         ),
-    )(hidden, own_kv, own_q, stored, cosine, sine, positions[:, None], done, key_pos)
+    )(hidden, own_kv, own_q, stored, cosine, sine, positions[None, :], done, done.reshape(1, -1), key_pos)
     attended = attended.transpose(1, 0, 2).reshape(row_count, local_heads, -1)
     cache = cache.transpose(1, 0, 2).reshape(row_count, local_heads, -1)
     return (attended, cache)

time: 338 us -> 318 us (0.941)
  Pallas kernels: 317 us -> 296 us
    pallas_call x1, Pallas kernels: 317 us -> 296 us  [local(): pl.pallas_call(functools.partial(kernel, n, groups, head_dev, hold_dev, l...]
    unnamed x18 -> x19, local copies, waits for them, and re-layouts: 12.3 us -> 11.2 us
where the time goes in v3:
time: 318 us
  Pallas kernels  296 us (93%)
  local copies, waits for them, and re-layouts  16.1 us (5%)
  other arithmetic  4.22 us (1%)
    pallas_call x1, Pallas kernels, local(): pl.pallas_call(functools.partial(kernel, n, groups, head_dev, hold_dev, l...  296 us
    unnamed x19, local copies, waits for them, and re-layouts  11.2 us

profile of v3, /device:TPU:0, one launch (start us, length us, event | category | flops | bytes accessed | tf_op | source)
XLA Modules:
  0.0 318.0 jit_solution(12725452791307069309)
XLA Ops:
  0.6 0.0 copy-start.1
  1.4 0.8 fusion.2
  2.3 0.1 or_convert_fusion
  2.3 0.1 broadcast_multiply_fusion.1
  2.4 0.7 broadcast_multiply_fusion
  3.1 0.1 broadcast_bitcast_fusion
  3.2 0.0 copy-start.3
  3.2 0.1 add_bitcast_fusion
  3.2 0.1 fusion.1
  3.3 0.6 copy.18
  3.9 1.1 copy.20
  5.0 1.3 copy.8
  6.3 1.0 copy.9
  7.3 1.3 broadcast_in_dim.5.kpos_ref
  8.6 0.0 copy-start
  8.6 1.9 fusion
  10.5 1.4 pad_maximum_fusion
  11.9 0.0 copy-done.1
  11.9 1.8 copy.15
  13.6 0.0 copy-done.3
  13.6 0.0 copy-done
  13.6 3.1 copy.16
  16.8 296.2 %shard_map.77 = (bf16[8,512,128]{2,1,0:T(8,128)(2,1)}, bf16[4,512,128]{2,1,0:T(8,128)(2,1)}) custom-call(bf16[512,8192]{1,0:T(8,128)(2,1)} %hidden_hbm.1, bf16[2048,512]{1,0:T(8,128)(2,1)} %bitcast.31, bf16[2048,1024]{1,0:T(8,128)(2,1)} %bitcast.30, bf16[4,512,128]{2,1,0:T(8,128)(2,1)} %bitcast.35, f32[1024,128]{1,0:T(8,128)} %get-tuple-element.15.cos_ref, ...), custom_call_target="tpu_custom_call" | custom-call | tf_op jit(solution)/shard_map/pallas_call | solution.py:558
  313.0 0.0 copy-start.2
  313.0 1.5 copy.11
  314.6 2.1 copy.13
  316.7 0.0 copy-done.2
  316.7 0.2 copy.12
  316.9 1.1 copy.14
  (4 shorter events, 0.0 us)
Async XLA Ops:
  0.6 11.2 %copy-start.1 = (bf16[2048,2,256]{2,1,0:T(2,128)(2,1)S(1)}, bf16[2048,2,256]{2,1,0:T(2,128)(2,1)}, u32[]{:S(2)}) copy-start(bf16[2048,2,256]{2,1,0:T(2,128)(2,1)} %param.10) | copy-start | bytes 6291460
  3.2 10.5 %copy-start.3 = (s32[1,1,4,256]{3,1,2,0:T(1,128)}, s32[1,1,4,256]{3,1,2,0:T(1,128)S(1)}, u32[]{:S(2)}) copy-start(s32[1,1,4,256]{3,1,2,0:T(1,128)S(1)} %copy.19) | copy-start | bytes 12292
  8.6 5.0 %copy-start = (bf16[2048,2,512]{2,1,0:T(2,128)(2,1)S(1)}, bf16[2048,2,512]{2,1,0:T(2,128)(2,1)}, u32[]{:S(2)}) copy-start(bf16[2048,2,512]{2,1,0:T(2,128)(2,1)} %param.9) | copy-start | bytes 12582916
  313.0 3.7 %copy-start.2 = (bf16[4,512,128]{2,1,0:T(8,128)(2,1)S(1)}, bf16[4,512,128]{2,1,0:T(8,128)(2,1)}, u32[]{:S(2)}) copy-start(bf16[4,512,128]{2,1,0:T(8,128)(2,1)} %get-tuple-element.5) | copy-start | bytes 1572868

commit v4 on v3

--- a/solution.py
+++ b/solution.py
@@ -182,15 +182,28 @@
         def _():
             down_copy(c, s, src).start()
 
+    def send_own_q(q):
+        at = pl.ds(pl.multiple_of(g * rest_part, 16), part)
+        src = own_q.at[at, columns(q)]
+
+        @pl.when(has_up)
+        def _():
+            up_copy(planes + q, s, src).start()
+
+        @pl.when(has_down)
+        def _():
+            down_copy(planes + q, s, src).start()
+
     def spread(c, o):
         for k in range(1, groups):
             side_copy(c, o, g, lax.rem(g + k, groups)).start()
 
-    def forward(c):
+    def forward(c, inner_done=False):
         def hop(d, _):
             lo, hi = s - d, s + d
-
-            @pl.when((lo >= 0) & ~idle)
+            first = (d == 1) & host & inner_done
+
+            @pl.when((lo >= 0) & ~idle & ~(first & (s == n - 2)))
             def _():
                 up_copy(c, lo).wait_recv()
 
@@ -200,7 +213,7 @@
 
                 spread(c, lo)
 
-            @pl.when((hi < n) & ~idle)
+            @pl.when((hi < n) & ~idle & ~(first & (s == 1)))
             def _():
                 down_copy(c, hi).wait_recv()
 
@@ -213,6 +226,11 @@
             return 0
 
         lax.fori_loop(1, n, hop, 0)
+
+    def inner_first(c):
+        o = jnp.where(s == 1, s + 1, s - 1)
+        down_copy(c, o).wait_recv()
+        spread(c, o)
 
     def kv_hop(j, d):
         lo, hi = s - d, s + d
@@ -349,12 +367,27 @@
             def _():
                 down_copy(c, s, src).start()
 
-        for c in range(chunks):
-            if c == planes:
-                for k in range(subs):
-                    lend_copy(k).start()
-                st_lend().start()
-            own_to_partner(c)
+        def own_sent(c):
+            @pl.when(s == 0)
+            def _():
+                up_copy(c, s).wait_send()
+
+            @pl.when(s == n - 1)
+            def _():
+                down_copy(c, s).wait_send()
+
+        order = [(functools.partial(own_to_partner, c), functools.partial(own_sent, c))
+                 for c in range(chunks)]
+        lent = [(lend_copy(k).start, lend_copy(k).wait_send) for k in range(subs)]
+        lent.append((st_lend().start, st_lend().wait_send))
+        order = order[:planes] + lent + order[planes:]
+        in_flight = 3
+        for i, (start, _) in enumerate(order):
+            if i >= in_flight:
+                order[i - in_flight][1]()
+            start()
+        for _, sent in order[-in_flight:]:
+            sent()
 
     for c in range(chunks):
         own_copy(c).wait()
@@ -367,10 +400,11 @@
             forward(2 * t)
             forward(2 * t + 1)
 
-        @pl.when(t == local_heads - 1)
-        def _():
-            for c in range(planes, chunks):
-                send_own(c)
+            def more(i, _):
+                send_own_q(t * group_size + i)
+                return 0
+
+            lax.fori_loop(0, group_size, more, 0)
 
         @pl.when(t >= 1)
         def _():
@@ -397,6 +431,8 @@
                 x_copy(k, hx, lax.rem(hx + i, head_dev)).start()
             for i in range(1, hold_dev):
                 mate_copy(k, hx, hc, lax.rem(hc + i, hold_dev)).start()
+            if k < heads:
+                inner_first(planes + k)
         for k in range(subs):
             for i in range(1, head_dev):
                 x = lax.rem(hx + i, head_dev)
@@ -416,11 +452,17 @@
 
         lax.fori_loop(0, local_heads, guest_planes, 0)
 
+        def inner_rest(c, _):
+            inner_first(c)
+            return 0
+
+        lax.fori_loop(planes + subs, chunks, inner_rest, 0)
+
     def late(t, _):
         @pl.when(t < heads // 2)
         def _():
-            forward(planes + 2 * t)
-            forward(planes + 2 * t + 1)
+            forward(planes + 2 * t, True)
+            forward(planes + 2 * t + 1, True)
 
         @pl.when(t >= 1)
         def _():
@@ -455,11 +497,11 @@
 
     def drain(c, _):
         def each(o, _):
-            @pl.when((has_up & (o <= s)) | ((s == 0) & (o == 0)))
+            @pl.when(has_up & (o <= s))
             def _():
                 up_copy(c, o).wait_send()
 
-            @pl.when((has_down & (o >= s)) | ((s == n - 1) & (o == n - 1)))
+            @pl.when(has_down & (o >= s))
             def _():
                 down_copy(c, o).wait_send()
 
@@ -515,9 +557,6 @@
 
     @pl.when(idle)
     def _():
-        for k in range(subs):
-            lend_copy(k).wait_send()
-        st_lend().wait_send()
         for q in range(heads):
             at = out_ref.at[q]
             remote(at, at, ret_send.at[q], ret_recv.at[q], seq=partner).wait_recv()

time: 318 us -> 324 us (1.019)
  Pallas kernels: 296 us -> 302 us
    pallas_call x1, Pallas kernels: 296 us -> 302 us  [local(): pl.pallas_call(functools.partial(kernel, n, groups, head_dev, hold_dev, l...]
where the time goes in v4:
time: 324 us
  Pallas kernels  302 us (93%)
  local copies, waits for them, and re-layouts  16.1 us (5%)
  other arithmetic  4.22 us (1%)
    pallas_call x1, Pallas kernels, local(): pl.pallas_call(functools.partial(kernel, n, groups, head_dev, hold_dev, l...  302 us
    unnamed x19, local copies, waits for them, and re-layouts  11.2 us

profile of v4, /device:TPU:0, one launch (start us, length us, event | category | flops | bytes accessed | tf_op | source)
XLA Modules:
  0.0 324.2 jit_solution(11773690316868277685)
XLA Ops:
  0.6 0.0 copy-start.1
  1.4 0.8 fusion.2
  2.3 0.1 or_convert_fusion
  2.3 0.1 broadcast_multiply_fusion.1
  2.4 0.7 broadcast_multiply_fusion
  3.1 0.1 broadcast_bitcast_fusion
  3.2 0.0 copy-start.3
  3.2 0.1 add_bitcast_fusion
  3.2 0.1 fusion.1
  3.3 0.6 copy.18
  3.9 1.1 copy.20
  5.0 1.3 copy.8
  6.3 1.0 copy.9
  7.3 1.3 broadcast_in_dim.5.kpos_ref
  8.6 0.0 copy-start
  8.6 1.9 fusion
  10.5 1.4 pad_maximum_fusion
  11.9 0.0 copy-done.1
  11.9 1.8 copy.15
  13.6 0.0 copy-done.3
  13.6 0.0 copy-done
  13.6 3.1 copy.16
  16.8 302.4 %shard_map.77 = (bf16[8,512,128]{2,1,0:T(8,128)(2,1)}, bf16[4,512,128]{2,1,0:T(8,128)(2,1)}) custom-call(bf16[512,8192]{1,0:T(8,128)(2,1)} %hidden_hbm.1, bf16[2048,512]{1,0:T(8,128)(2,1)} %bitcast.31, bf16[2048,1024]{1,0:T(8,128)(2,1)} %bitcast.30, bf16[4,512,128]{2,1,0:T(8,128)(2,1)} %bitcast.35, f32[1024,128]{1,0:T(8,128)} %get-tuple-element.15.cos_ref, ...), custom_call_target="tpu_custom_call" | custom-call | tf_op jit(solution)/shard_map/pallas_call | solution.py:597
  319.2 0.0 copy-start.2
  319.2 1.5 copy.11
  320.8 2.1 copy.13
  322.9 0.0 copy-done.2
  322.9 0.2 copy.12
  323.1 1.1 copy.14
  (4 shorter events, 0.0 us)
Async XLA Ops:
  0.6 11.2 %copy-start.1 = (bf16[2048,2,256]{2,1,0:T(2,128)(2,1)S(1)}, bf16[2048,2,256]{2,1,0:T(2,128)(2,1)}, u32[]{:S(2)}) copy-start(bf16[2048,2,256]{2,1,0:T(2,128)(2,1)} %param.10) | copy-start | bytes 6291460
  3.2 10.5 %copy-start.3 = (s32[1,1,4,256]{3,1,2,0:T(1,128)}, s32[1,1,4,256]{3,1,2,0:T(1,128)S(1)}, u32[]{:S(2)}) copy-start(s32[1,1,4,256]{3,1,2,0:T(1,128)S(1)} %copy.19) | copy-start | bytes 12292
  8.6 5.0 %copy-start = (bf16[2048,2,512]{2,1,0:T(2,128)(2,1)S(1)}, bf16[2048,2,512]{2,1,0:T(2,128)(2,1)}, u32[]{:S(2)}) copy-start(bf16[2048,2,512]{2,1,0:T(2,128)(2,1)} %param.9) | copy-start | bytes 12582916
  319.2 3.7 %copy-start.2 = (bf16[4,512,128]{2,1,0:T(8,128)(2,1)S(1)}, bf16[4,512,128]{2,1,0:T(8,128)(2,1)}, u32[]{:S(2)}) copy-start(bf16[4,512,128]{2,1,0:T(8,128)(2,1)} %get-tuple-element.5) | copy-start | bytes 1572868

commit v5 on v4

--- a/solution.py
+++ b/solution.py
@@ -203,7 +203,7 @@
             lo, hi = s - d, s + d
             first = (d == 1) & host & inner_done
 
-            @pl.when((lo >= 0) & ~idle & ~(first & (s == n - 2)))
+            @pl.when((lo >= 0) & ~idle & ~first)
             def _():
                 up_copy(c, lo).wait_recv()
 
@@ -213,7 +213,7 @@
 
                 spread(c, lo)
 
-            @pl.when((hi < n) & ~idle & ~(first & (s == 1)))
+            @pl.when((hi < n) & ~idle & ~first)
             def _():
                 down_copy(c, hi).wait_recv()
 
@@ -226,6 +226,20 @@
             return 0
 
         lax.fori_loop(1, n, hop, 0)
+
+    def outer_first(c):
+        o = guest
+        up_copy(c, o).wait_recv()
+
+        @pl.when(s == 1)
+        def _():
+            up_copy(c, o).start()
+
+        @pl.when(s == n - 2)
+        def _():
+            down_copy(c, o).start()
+
+        spread(c, o)
 
     def inner_first(c):
         o = jnp.where(s == 1, s + 1, s - 1)
@@ -451,6 +465,8 @@
             return 0
 
         lax.fori_loop(0, local_heads, guest_planes, 0)
+        outer_first(planes)
+        outer_first(planes + 1)
 
         def inner_rest(c, _):
             inner_first(c)
@@ -459,6 +475,11 @@
         lax.fori_loop(planes + subs, chunks, inner_rest, 0)
 
     def late(t, _):
+        @pl.when((t + 1 < heads // 2) & host)
+        def _():
+            outer_first(planes + 2 * t + 2)
+            outer_first(planes + 2 * t + 3)
+
         @pl.when(t < heads // 2)
         def _():
             forward(planes + 2 * t, True)

time: 324 us -> 306 us (0.944)
  Pallas kernels: 302 us -> 283 us
    pallas_call x1, Pallas kernels: 302 us -> 283 us  [local(): pl.pallas_call(functools.partial(kernel, n, groups, head_dev, hold_dev, l...]
where the time goes in v5:
time: 306 us; the launch traced here: 305 us
  Pallas kernels  283 us (92%)
  local copies, waits for them, and re-layouts  16.1 us (5%)
  other arithmetic  4.22 us (1%)
    pallas_call x1, Pallas kernels, local(): pl.pallas_call(functools.partial(kernel, n, groups, head_dev, hold_dev, l...  283 us
    unnamed x19, local copies, waits for them, and re-layouts  11.2 us

profile of v5, /device:TPU:0, one launch (start us, length us, event | category | flops | bytes accessed | tf_op | source)
XLA Modules:
  0.0 305.2 jit_solution(8753310414870906705)
XLA Ops:
  0.6 0.0 copy-start.1
  1.4 0.8 fusion.2
  2.3 0.1 or_convert_fusion
  2.3 0.1 broadcast_multiply_fusion.1
  2.4 0.7 broadcast_multiply_fusion
  3.1 0.1 broadcast_bitcast_fusion
  3.2 0.0 copy-start.3
  3.2 0.1 add_bitcast_fusion
  3.2 0.1 fusion.1
  3.3 0.6 copy.18
  3.9 1.1 copy.20
  5.0 1.3 copy.8
  6.3 1.0 copy.9
  7.3 1.3 broadcast_in_dim.5.kpos_ref
  8.6 0.0 copy-start
  8.6 1.9 fusion
  10.5 1.4 pad_maximum_fusion
  11.9 0.0 copy-done.1
  11.9 1.8 copy.15
  13.6 0.0 copy-done.3
  13.6 0.0 copy-done
  13.6 3.1 %copy.16 = bf16[256,8,2,512]{3,1,2,0:T(8,128)(2,1)} copy(bf16[256,8,2,512]{3,2,1,0:T(2,128)(2,1)S(1)} %bitcast.32) | data formatting | bytes 8388608
  16.8 283.4 %shard_map.77 = (bf16[8,512,128]{2,1,0:T(8,128)(2,1)}, bf16[4,512,128]{2,1,0:T(8,128)(2,1)}) custom-call(bf16[512,8192]{1,0:T(8,128)(2,1)} %hidden_hbm.1, bf16[2048,512]{1,0:T(8,128)(2,1)} %bitcast.31, bf16[2048,1024]{1,0:T(8,128)(2,1)} %bitcast.30, bf16[4,512,128]{2,1,0:T(8,128)(2,1)} %bitcast.35, f32[1024,128]{1,0:T(8,128)} %get-tuple-element.15.cos_ref, ...), custom_call_target="tpu_custom_call" | custom-call | tf_op jit(solution)/shard_map/pallas_call | solution.py:618
  300.2 0.0 copy-start.2
  300.2 1.5 copy.11
  301.7 2.1 copy.13
  303.8 0.0 copy-done.2
  303.8 0.2 copy.12
  304.1 1.1 copy.14
  (4 shorter events, 0.0 us)
Async XLA Ops:
  0.6 11.2 %copy-start.1 = (bf16[2048,2,256]{2,1,0:T(2,128)(2,1)S(1)}, bf16[2048,2,256]{2,1,0:T(2,128)(2,1)}, u32[]{:S(2)}) copy-start(bf16[2048,2,256]{2,1,0:T(2,128)(2,1)} %param.10) | copy-start | bytes 6291460
  3.2 10.5 %copy-start.3 = (s32[1,1,4,256]{3,1,2,0:T(1,128)}, s32[1,1,4,256]{3,1,2,0:T(1,128)S(1)}, u32[]{:S(2)}) copy-start(s32[1,1,4,256]{3,1,2,0:T(1,128)S(1)} %copy.19) | copy-start | bytes 12292
  8.6 5.0 %copy-start = (bf16[2048,2,512]{2,1,0:T(2,128)(2,1)S(1)}, bf16[2048,2,512]{2,1,0:T(2,128)(2,1)}, u32[]{:S(2)}) copy-start(bf16[2048,2,512]{2,1,0:T(2,128)(2,1)} %param.9) | copy-start | bytes 12582916
  300.2 3.7 %copy-start.2 = (bf16[4,512,128]{2,1,0:T(8,128)(2,1)S(1)}, bf16[4,512,128]{2,1,0:T(8,128)(2,1)}, u32[]{:S(2)}) copy-start(bf16[4,512,128]{2,1,0:T(8,128)(2,1)} %get-tuple-element.5) | copy-start | bytes 1572868
